TPU v7x, 32 devices: a whole 2x2x4 slice. The times are simulated.
32 devices in a mesh: grp: 2 (over x), tile: 8 (over z, y), tm: 2 (over core).
Axes of the slice: x: 2, y: 2, z: 4, core: 2. Of those that a mesh axis runs over, the one named last changes fastest.
Arguments:
- forcing: bfloat16 [24, 64, 32, 1024], P('tm', 'tile', 'grp'), parts along dimension 2, may hold values from -6 to 6
- first_weight: bfloat16 [3, 3, 16, 64], replicated, may hold values from -0.5 to 0.5
- second_weight: bfloat16 [3, 3, 64, 64], replicated, may hold values from -0.25 to 0.25
- head_weight: bfloat16 [64], replicated, may hold values from -0.75 to 0.75
- flow_codes: int32 [128, 1024], P('grp', 'tile'), parts along dimension 0, may hold values from 0 to 3, as said below
- outlet_cells: int32 [8, 64], P('tile', 'grp'), parts along dimension 1, may hold values from 127 to 8191, as said below
- receivers: int32 [8, 64], P('tile', 'grp'), parts along dimension 1, may hold values from -1 to 7, as said below
- inlet_cells: int32 [8, 64], P('tile', 'grp'), parts along dimension 1, may hold values from -1 to 8191, as said below
- levels: int32 [16], P(('grp', 'tile')), parts along dimension 0, may hold values from 0 to 7, as said below
Outputs:
- runoff: bfloat16 [24, 128, 1024], P('tm', 'grp', 'tile'), parts along dimension 1
- discharge: float32 [8, 64, 24], P('tile', 'grp', 'tm'), parts along dimension 1
There are 2 independent parts, one for each index of `grp`. A program takes and returns all parts, laid end to end along the dimension named above; an argument that names none is the same for every part. Nothing has to cross between parts.
Inputs may be any that keep to these rules, and one draw needn't show every extreme that they name: `flow_codes`: in the last row of every tile each code is 0; elsewhere codes are 1, 2 or 3. `outlet_cells`: A tile's outlets are distinct cells of its last row; the last column's cell is always one. `receivers`: each outlet of a tile of level p below 7 sends to a tile of level p + 1; outlets of top-level tiles send to -1. `inlet_cells`: -1 exactly where receivers is -1. `levels`: every level holds 1 tiles.
All inputs are finite; a program needn't handle non-finite values.
Results may differ from a plain program's by a relative error of at most 0.0034.
Values may be sent and summed in bfloat16 or wider, within the bound.
A program may use at most 128 MiB of HBM per device.

v0:
```python
from functools import partial

import jax
import jax.numpy as jnp
from jax import lax
from jax.sharding import PartitionSpec as P

LEVELS = 8


column_moves = (1, 1, 0, -1, -1, -1, 0, 1)
row_moves = (0, 1, 1, 1, 0, -1, -1, -1)


def padded(value, sides, width):
    for axis, dim in sides:
        count, length = (lax.axis_size(axis), value.shape[dim])
        up = [(i, (i + 1) % count) for i in range(count - 1)]
        down = [(j, i) for i, j in up]
        last = lax.slice_in_dim(value, length - width, length, axis=dim)
        first = lax.slice_in_dim(value, 0, width, axis=dim)
        before = lax.ppermute(last, axis, up)
        after = lax.ppermute(first, axis, down)
        value = jnp.concatenate([before, value, after], axis=dim)
    return value


def lookup_table(direction, table):
    running = jnp.zeros(direction.shape, jnp.int32)
    for code_value in range(8):
        running = running + jnp.where(direction == code_value, table[code_value], 0).astype(
            jnp.int32
        )
    return running


def drain_roots(direction, outlets):
    tile_width, tile_height = direction.shape
    column_ids = lax.broadcasted_iota(jnp.int32, direction.shape, 0)
    row_ids = lax.broadcasted_iota(jnp.int32, direction.shape, 1)
    new_column = column_ids + lookup_table(direction, column_moves)
    new_row = row_ids + lookup_table(direction, row_moves)
    inside = (
        (new_column >= 0) & (new_column < tile_width) & (new_row >= 0) & (new_row < tile_height)
    )
    own_cells = (column_ids * tile_height + row_ids).reshape(-1)
    moved = jnp.where(
        inside, new_column * tile_height + new_row, column_ids * tile_height + row_ids
    ).reshape(-1)
    is_outlet = jnp.any(own_cells[:, None] == outlets[None, :], axis=1)
    moved = jnp.where(is_outlet, own_cells, moved)
    for turn_index in range((tile_width + tile_height).bit_length()):
        moved = moved[moved]
    return moved


def edge_mask(column_count, row_count, left_out, right_out):
    column_ids = lax.broadcasted_iota(jnp.int32, (column_count, 1, row_count), 0)
    row_ids = lax.broadcasted_iota(jnp.int32, (column_count, 1, row_count), 2)
    outside = (column_ids == 0) & left_out | (column_ids == column_count - 1) & right_out
    outside = outside | (row_ids == 0) & True | (row_ids == row_count - 1) & True
    return jnp.where(outside, 0.0, 1.0).astype(jnp.float32)


def tap_sum(source, weights):
    out_columns = source.shape[0] - 2
    out_rows = source.shape[2] - 2
    running = jnp.zeros((out_columns, weights.shape[3], out_rows), jnp.float32)
    for column_tap in range(3):
        for row_tap in range(3):
            window_cut = source[
                column_tap : column_tap + out_columns, :, row_tap : row_tap + out_rows
            ]
            running = running + jnp.einsum(
                "wir,io->wor",
                window_cut,
                weights[column_tap, row_tap],
                preferred_element_type=jnp.float32,
            )
    return running


def conv_layers(first_weight, second_weight, head_weight, keep_mask, framed):
    hidden = (jnp.maximum(tap_sum(framed, first_weight), 0.0) * keep_mask).astype(jnp.bfloat16)
    deep = jnp.maximum(tap_sum(hidden, second_weight), 0.0)
    logits = jnp.sum(deep * head_weight.astype(jnp.float32)[None, :, None], axis=1)
    return jax.nn.softplus(logits).astype(jnp.bfloat16)


def local(
    forcing,
    first_weight,
    second_weight,
    head_weight,
    flow_codes,
    outlet_cells,
    receivers,
    inlet_cells,
    levels,
):
    tile_count = lax.axis_size("tile")
    tile_place = lax.axis_index("tile")
    at_first = tile_place == 0
    at_last = tile_place == tile_count - 1
    framed = padded(forcing, (("tile", 1),), 2)
    framed = jnp.pad(framed, ((0, 0), (0, 0), (0, 0), (2, 2)))
    keep_mask = edge_mask(framed.shape[1] - 2, framed.shape[3] - 2, at_first, at_last)
    band_runoff = lax.map(
        partial(conv_layers, first_weight, second_weight, head_weight, keep_mask), framed
    )
    runoff = lax.all_to_all(band_runoff, "tile", split_axis=2, concat_axis=1, tiled=True)
    step_count = runoff.shape[0]
    outlets_here = outlet_cells[0]
    outlet_count = outlets_here.shape[0]
    root_cells = drain_roots(flow_codes, outlets_here)
    member = (root_cells[:, None] == outlets_here[None, :]).astype(jnp.bfloat16)
    local_flow = jnp.dot(
        runoff.reshape(step_count, -1), member, preferred_element_type=jnp.float32
    ).T
    peer_ids = lax.broadcasted_iota(jnp.int32, (tile_count, outlet_count), 0)
    queries = jnp.where(receivers[0][None, :] == peer_ids, inlet_cells[0][None, :], -1)
    incoming = lax.all_to_all(queries, "tile", split_axis=0, concat_axis=0, tiled=True).reshape(-1)
    safe_cells = jnp.maximum(incoming, 0)
    inlet_roots = root_cells[safe_cells]
    drains_to = (inlet_roots[:, None] == outlets_here[None, :]) & (incoming[:, None] >= 0)
    inflow_table = drains_to.astype(jnp.float32)
    outflow = local_flow
    for level_now in range(LEVELS - 1):
        sent_flow = jnp.where(levels[0] == level_now, outflow, 0.0)
        everyone = lax.all_gather(sent_flow, "tile", axis=0, tiled=True)
        outflow = outflow + jnp.einsum(
            "ko,ks->os", inflow_table, everyone, precision=lax.Precision.HIGHEST
        )
    cell_count = flow_codes.shape[0] * flow_codes.shape[1]
    discharge = (outflow * (outlet_count / cell_count))[None]
    return (runoff, discharge)


def solution(mesh):
    placed = (
        P("tm", "tile", "grp", None),
        P(),
        P(),
        P(),
        P("grp", "tile"),
        P("tile", "grp"),
        P("tile", "grp"),
        P("tile", "grp"),
        P(("grp", "tile")),
    )
    return jax.shard_map(
        local,
        mesh=mesh,
        in_specs=placed,
        out_specs=(P("tm", "grp", "tile"), P("tile", "grp", "tm")),
        check_vma=False,
    )
```

profile of v0, /device:TPU:0, one launch (start us, length us, event | category | flops | bytes accessed | tf_op | source)
XLA Modules:
  0.0 779.8 jit_solution(8231828621778076772)
XLA Ops:
  0.7 2.8 fusion.117
  4.7 6.4 collective-permute-start
  11.7 5.4 all-to-all-start.1
  17.6 45.5 %gather_fusion = s32[8192]{0:T(1024)S(1)} fusion(s32[8192]{0:T(1024)S(1)} %get-tuple-element.147, s32[8192]{0:T(1024)S(1)} %broadcast_clamp_fusion.7), kind=kCustom, calls=%fused_computation | custom fusion | bytes 98304 | tf_op jit(solution)/shard_map/gather | solution.py:53
  63.2 45.5 %gather_fusion.1 = s32[8192]{0:T(1024)S(1)} fusion(s32[8192]{0:T(1024)S(1)} %gather_fusion, s32[8192]{0:T(1024)S(1)} %broadcast_clamp_fusion.6), kind=kCustom, calls=%fused_computation.1 | custom fusion | bytes 98304 | tf_op jit(solution)/shard_map/gather | solution.py:53
  108.8 45.5 %gather_fusion.2 = s32[8192]{0:T(1024)S(1)} fusion(s32[8192]{0:T(1024)S(1)} %gather_fusion.1, s32[8192]{0:T(1024)S(1)} %broadcast_clamp_fusion.5), kind=kCustom, calls=%fused_computation.2 | custom fusion | bytes 98304 | tf_op jit(solution)/shard_map/gather | solution.py:53
  154.4 45.5 %gather_fusion.3 = s32[8192]{0:T(1024)S(1)} fusion(s32[8192]{0:T(1024)S(1)} %gather_fusion.2, s32[8192]{0:T(1024)S(1)} %broadcast_clamp_fusion.4), kind=kCustom, calls=%fused_computation.3 | custom fusion | bytes 98304 | tf_op jit(solution)/shard_map/gather | solution.py:53
  200.0 45.5 %gather_fusion.4 = s32[8192]{0:T(1024)S(1)} fusion(s32[8192]{0:T(1024)S(1)} %gather_fusion.3, s32[8192]{0:T(1024)S(1)} %broadcast_clamp_fusion.3), kind=kCustom, calls=%fused_computation.4 | custom fusion | bytes 98304 | tf_op jit(solution)/shard_map/gather | solution.py:53
  245.6 45.5 %gather_fusion.5 = s32[8192]{0:T(1024)S(1)} fusion(s32[8192]{0:T(1024)S(1)} %gather_fusion.4, s32[8192]{0:T(1024)S(1)} %broadcast_clamp_fusion.2), kind=kCustom, calls=%fused_computation.5 | custom fusion | bytes 98304 | tf_op jit(solution)/shard_map/gather | solution.py:53
  291.2 45.5 %gather_fusion.6 = s32[8192]{0:T(1024)S(1)} fusion(s32[8192]{0:T(1024)S(1)} %gather_fusion.5, s32[8192]{0:T(1024)S(1)} %broadcast_clamp_fusion.1), kind=kCustom, calls=%fused_computation.6 | custom fusion | bytes 98304 | tf_op jit(solution)/shard_map/gather | solution.py:53
  337.1 6.0 fusion.80
  343.1 149.4 %while.11 = (s32[]{:T(128)}, bf16[12,8,1024]{2,1,0:T(8,128)(2,1)}, bf16[12,12,16,1028]{3,2,1,0:T(8,128)(2,1)}, bf16[3,3,16,64]{3,2,1,0:T(8,128)(2,1)S(1)}, bf16[...) while((s32[]{:T(128)}, bf16[12,8,1024]{2,1,0:T(8,128)(2,1)}, ...), condition=%wide.region_2.3_spmd.clone, body=%wide.region_0.2_spmd.clone.sunk | while | flops 806162304 | bytes 93401688 | solution.py:108
  353.8 1.3 multiply_reduce_fusion.2
  366.2 1.3 multiply_reduce_fusion.2
  391.1 1.3 multiply_reduce_fusion.2
  403.5 1.3 multiply_reduce_fusion.2
  415.9 1.3 multiply_reduce_fusion.2
  440.8 1.3 multiply_reduce_fusion.2
  453.3 1.3 multiply_reduce_fusion.2
  492.6 2.6 copy.56
  495.1 5.0 reshape.475
  500.1 6.0 all-to-all-start
  506.2 45.5 %gather_fusion.7 = s32[8192]{0:T(1024)S(1)} fusion(s32[8192]{0:T(1024)S(1)} %gather_fusion.6, s32[8192]{0:T(1024)S(1)} %broadcast_clamp_fusion), kind=kCustom, calls=%fused_computation.7 | custom fusion | bytes 98304 | tf_op jit(solution)/shard_map/gather | solution.py:53
  553.9 1.7 gather_fusion.8
  555.7 4.9 reshape.476
  562.5 31.1 %all-gather = f32[8,32,12]{1,2,0:T(8,128)S(1)} all-gather(f32[1,32,12]{1,2,0:T(8,128)S(1)} %select_bitcast_fusion.7), channel_id=1, replica_groups=mesh['grp'=2,'tile'=8,'tm'=2] {'tile'}, dimensions={0}, use_global_device_ids=true | all-gather | bytes 13824 | tf_op jit(solution)/shard_map/all_gather | solution.py:130
  593.9 30.5 %all-gather.1 = f32[8,32,12]{1,2,0:T(8,128)S(1)} all-gather(f32[1,32,12]{1,2,0:T(8,128)S(1)} %select_bitcast_fusion.6), channel_id=1, replica_groups=mesh['grp'=2,'tile'=8,'tm'=2] {'tile'}, dimensions={0}, use_global_device_ids=true | all-gather | bytes 13824 | tf_op jit(solution)/shard_map/all_gather | solution.py:130
  624.8 30.5 %all-gather.2 = f32[8,32,12]{1,2,0:T(8,128)S(1)} all-gather(f32[1,32,12]{1,2,0:T(8,128)S(1)} %select_bitcast_fusion.5), channel_id=1, replica_groups=mesh['grp'=2,'tile'=8,'tm'=2] {'tile'}, dimensions={0}, use_global_device_ids=true | all-gather | bytes 13824 | tf_op jit(solution)/shard_map/all_gather | solution.py:130
  655.7 30.5 %all-gather.3 = f32[8,32,12]{1,2,0:T(8,128)S(1)} all-gather(f32[1,32,12]{1,2,0:T(8,128)S(1)} %select_bitcast_fusion.4), channel_id=1, replica_groups=mesh['grp'=2,'tile'=8,'tm'=2] {'tile'}, dimensions={0}, use_global_device_ids=true | all-gather | bytes 13824 | tf_op jit(solution)/shard_map/all_gather | solution.py:130
  686.5 30.5 %all-gather.4 = f32[8,32,12]{1,2,0:T(8,128)S(1)} all-gather(f32[1,32,12]{1,2,0:T(8,128)S(1)} %select_bitcast_fusion.3), channel_id=1, replica_groups=mesh['grp'=2,'tile'=8,'tm'=2] {'tile'}, dimensions={0}, use_global_device_ids=true | all-gather | bytes 13824 | tf_op jit(solution)/shard_map/all_gather | solution.py:130
  717.4 30.5 %all-gather.5 = f32[8,32,12]{1,2,0:T(8,128)S(1)} all-gather(f32[1,32,12]{1,2,0:T(8,128)S(1)} %select_bitcast_fusion.2), channel_id=1, replica_groups=mesh['grp'=2,'tile'=8,'tm'=2] {'tile'}, dimensions={0}, use_global_device_ids=true | all-gather | bytes 13824 | tf_op jit(solution)/shard_map/all_gather | solution.py:130
  748.3 30.5 %all-gather.6 = f32[8,32,12]{1,2,0:T(8,128)S(1)} all-gather(f32[1,32,12]{1,2,0:T(8,128)S(1)} %select_bitcast_fusion.1), channel_id=1, replica_groups=mesh['grp'=2,'tile'=8,'tm'=2] {'tile'}, dimensions={0}, use_global_device_ids=true | all-gather | bytes 13824 | tf_op jit(solution)/shard_map/all_gather | solution.py:130
  (345 shorter events, 147.8 us)
Async XLA Ops:
  0.6 10.5 %copy-start.5 = (s32[1,32]{1,0:T(1,128)S(1)}, s32[1,32]{1,0:T(1,128)}, u32[]{:S(2)}) copy-start(s32[1,32]{1,0:T(1,128)} %param.18) | copy-start | bytes 388
  0.6 10.5 %copy-start.6 = (s32[1,32]{1,0:T(1,128)S(1)}, s32[1,32]{1,0:T(1,128)}, u32[]{:S(2)}) copy-start(s32[1,32]{1,0:T(1,128)} %param.17) | copy-start | bytes 388
  0.7 16.6 %copy-start.7 = (s32[1,32]{1,0:T(1,128)S(1)}, s32[1,32]{1,0:T(1,128)}, u32[]{:S(2)}) copy-start(s32[1,32]{1,0:T(1,128)} %param.16) | copy-start | bytes 388
  0.7 16.8 %copy-start.4 = (s32[64,128]{1,0:T(8,128)S(1)}, s32[64,128]{1,0:T(8,128)}, u32[]{:S(2)}) copy-start(s32[64,128]{1,0:T(8,128)} %param.15) | copy-start | bytes 98308
  3.4 333.6 %collective-permute-start.1 = (bf16[12,2,16,1024]{3,2,1,0:T(8,128)(2,1)}, bf16[12,2,16,1024]{3,2,1,0:T(8,128)(2,1)}, u32[]{:S(2)}, u32[]{:S(2)}) collective-permute-start(bf16[12,2,16,1024]{3,2,1,0:T(8,128)(2,1)} %get-tuple-element.150), channel_id=1, source_target_pairs={{2,0},{4,2},{6,4},{8,6},{10,8},{12,10},{14,12},{3,1},{5,3},{7,5},{... | collective-permute-start | bytes 2359304 | tf_op jit(solution)/shard_map/ppermute | solution.py:23
  4.7 332.4 %collective-permute-start = (bf16[12,2,16,1024]{3,2,1,0:T(8,128)(2,1)}, bf16[12,2,16,1024]{3,2,1,0:T(8,128)(2,1)}, u32[]{:S(2)}, u32[]{:S(2)}) collective-permute-start(bf16[12,2,16,1024]{3,2,1,0:T(8,128)(2,1)} %get-tuple-element.149), channel_id=1, source_target_pairs={{0,2},{2,4},{4,6},{6,8},{8,10},{10,12},{12,14},{1,3},{3,5},{5,7},{... | collective-permute-start | bytes 2359304 | tf_op jit(solution)/shard_map/ppermute | solution.py:22
  11.7 488.4 %all-to-all-start.1 = ((s32[8,1,32]{2,1,0:T(1,128)}), s32[8,1,32]{2,1,0:T(1,128)}, u32[]{:S(2)}, u32[]{:S(2)}) async-start(s32[8,1,32]{2,1,0:T(1,128)} %compare_select_fusion.9), calls=%async_computation.1 | async-start | bytes 8192 | tf_op jit(solution)/shard_map/all_to_all | solution.py:122
  291.2 45.6 %copy-start.3 = (bf16[3,3,64,64]{3,2,1,0:T(8,128)(2,1)S(1)}, bf16[3,3,64,64]{3,2,1,0:T(8,128)(2,1)}, u32[]{:S(2)}) copy-start(bf16[3,3,64,64]{3,2,1,0:T(8,128)(2,1)} %param.13) | copy-start | bytes 221188
  291.2 45.9 %copy-start = (bf16[12,8,16,1024]{3,2,1,0:T(8,128)(2,1)S(1)}, bf16[12,8,16,1024]{3,2,1,0:T(8,128)(2,1)}, u32[]{:S(2)}) copy-start(bf16[12,8,16,1024]{3,2,1,0:T(8,128)(2,1)} %param.11) | copy-start | bytes 9437188
  337.0 6.1 copy-start.1
  337.1 6.1 copy-start.9
  500.1 55.5 %all-to-all-start = ((bf16[8,2,6144]{2,1,0:T(2,128)(2,1)}), bf16[8,2,6144]{2,1,0:T(2,128)(2,1)S(1)}, u32[]{:S(2)}, u32[]{:S(2)}) async-start(bf16[8,2,6144]{2,1,0:T(2,128)(2,1)} %reshape.475), calls=%async_computation | async-start | bytes 393216 | tf_op jit(solution)/shard_map/all_to_all | solution.py:111
  555.7 6.4 copy-start.8
  561.9 217.9 %copy-start.2 = (bf16[12,8,8,128]{3,1,2,0:T(8,128)(2,1)}, bf16[12,8,8,128]{3,1,2,0:T(8,128)(2,1)S(1)}, u32[]{:S(2)}) copy-start(bf16[12,8,8,128]{3,1,2,0:T(8,128)(2,1)S(1)} %copy.57) | copy-start | bytes 589828
where the time goes:
time: 781 us; the launch traced here: 780 us
  local copies, waits for them, and re-layouts  397 us (51%)
  blocking collectives  214 us (27%)
  matrix products  129 us (17%)
  starting transfers between devices  19.1 us (2%)
  other arithmetic  17.5 us (2%)
    gather x8, local copies, waits for them, and re-layouts, drain_roots(): moved = moved[moved]  364 us
    all_gather x7, blocking collectives, local(): everyone = lax.all_gather(sent_flow, 'tile', axis=0, tiled=True)  214 us
    dot_general x216, matrix products, tap_sum(): jnp.einsum('wir,io->wor', window_cut, weights[column_tap, row_tap], prefe...  127 us
  transfers between devices with their start and end apart: 4, of which 0 were waited for; matrix products, arithmetic and copies ran while one was open for 68% of the time, Pallas kernels for 0%

commit v1 on v0

v1 whole, which is shorter than its diff:
```python
from functools import partial

import jax
import jax.numpy as jnp
from jax import lax
from jax.experimental import pallas as pl
from jax.experimental.pallas import tpu as pltpu
from jax.sharding import PartitionSpec as P

LEVELS = 8
F32 = jnp.float32
BF16 = jnp.bfloat16
VMEM_BYTES = 56 * 1024 * 1024


def iota(shape, dim):
    return lax.broadcasted_iota(jnp.int32, shape, dim)


def as_column(row_value, count):
    spread = jnp.broadcast_to(row_value.astype(F32), (count, count))
    return jnp.sum(
        jnp.where(iota((count, count), 0) == iota((count, count), 1), spread, 0.0),
        axis=1,
        keepdims=True,
    )


def drain_kernel(codes_ref, outlets_ref, receivers_ref, inlets_ref, levels_ref, packed_ref):
    width, height = codes_ref.shape
    count = outlets_ref.shape[1]
    codes = codes_ref[...].astype(F32)
    codes = jnp.concatenate([codes, jnp.full((height - width, height), 2.0, F32)], axis=0)
    codes = codes.T.astype(jnp.int32)
    shape = (height, height)
    rows, columns = iota(shape, 0), iota(shape, 1)
    moved = columns + jnp.where(codes == 1, 1, 0) - jnp.where(codes == 3, 1, 0)
    moved = jnp.where((moved < 0) | (moved >= width), height - 1, moved)
    landing = jnp.where((rows == height - 1) | (columns >= width), columns, moved)
    reach = 1
    while reach < height:
        below = jnp.concatenate([landing[reach:], columns[:reach]], axis=0)
        landing = jnp.take_along_axis(below, landing, axis=1, mode="promise_in_bounds")
        reach *= 2
    outlet_columns = as_column(outlets_ref[...], count).astype(jnp.int32) // height
    lanes = iota((count, height), 1)
    ranked = jnp.where(
        outlet_columns >= lanes, outlet_columns * count + iota((count, height), 0), height * count
    )
    nearest = jnp.min(ranked.astype(F32), axis=0, keepdims=True).astype(jnp.int32)
    nearest = jnp.where(iota((1, height), 1) < width, nearest % count, -1)
    drained = jnp.take_along_axis(
        jnp.broadcast_to(nearest, shape), landing, axis=1, mode="promise_in_bounds"
    )
    packed_ref[:width, :] = drained.astype(F32).T[:width]
    lane = iota((count, height), 1)
    table = jnp.where(lane == 0, as_column(receivers_ref[...], count), 0.0)
    table = jnp.where(lane == 1, as_column(inlets_ref[...], count), table)
    table = jnp.where(lane == 2, levels_ref[0].astype(F32), table)
    packed_ref[width:, :] = table


def shifted(value):
    count = value.shape[1]
    lanes = iota(value.shape, 1)
    before = jnp.where(lanes == 0, 0.0, pltpu.roll(value, 1, 1))
    after = jnp.where(lanes == count - 1, 0.0, pltpu.roll(value, count - 1, 1))
    return before, value, after


def route_matrix(gathered_ref, width, count):
    tiles, depth, height = gathered_ref.shape
    everything = tiles * count
    table = gathered_ref[:, width:, :].reshape(everything, height)
    receiver = table[:, 0:1].astype(jnp.int32)
    inlet = table[:, 1:2].astype(jnp.int32)
    sends = (receiver >= 0) & (table[:, 2:3] < LEVELS - 1.0)
    inlet_column = jnp.maximum(inlet, 0) // height
    inlet_row = jnp.maximum(inlet, 0) % height
    drained = gathered_ref[:, :width, :].reshape(tiles * width, height).astype(BF16)
    picks = jnp.where(
        iota((everything, tiles * width), 1) == receiver * width + inlet_column, 1.0, 0.0
    ).astype(BF16)
    picked = jnp.dot(picks, drained, preferred_element_type=F32)
    entered = jnp.sum(
        jnp.where(iota(picked.shape, 1) == inlet_row, picked, 0.0), axis=1, keepdims=True
    ).astype(jnp.int32)
    target = jnp.where(sends & (entered >= 0), receiver * count + entered, -1)
    square = (everything, everything)
    hop = jnp.where(iota(square, 1) == target, 1.0, 0.0)
    passed = hop + jnp.where(iota(square, 0) == iota(square, 1), 1.0, 0.0)
    hops = 1
    hop = hop.astype(BF16)
    while 2 * hops < LEVELS:
        hop = jnp.dot(hop, hop, preferred_element_type=F32).astype(BF16)
        passed = passed + jnp.dot(passed.astype(BF16), hop, preferred_element_type=F32)
        hops *= 2
    return passed


def conv_kernel(
    count,
    group1,
    group2,
    before_ref,
    forcing_ref,
    after_ref,
    w1_ref,
    w2_ref,
    head_ref,
    gathered_ref,
    runoff_ref,
    flow_ref,
    x_ref,
    h_ref,
    s_ref,
):
    step = pl.program_id(0)
    place = lax.axis_index("tile")
    tiles = runoff_ref.shape[0]
    _, band, cin, rows = forcing_ref.shape
    height = runoff_ref.shape[3]
    channels = head_ref.shape[0]
    chunk = 256
    first = 0
    for ref in (before_ref, forcing_ref, after_ref):
        depth = ref.shape[1] * cin
        parts = shifted(ref[0].reshape(depth, rows).astype(F32))
        for b in range(3):
            x_ref[b, first : first + depth, :] = parts[b].astype(BF16)
        first += depth
    start = 0
    while start < band + 2:
        wide = min(group1, band + 2 - start)
        span = (wide + 2) * cin
        if wide == group1:
            weights = w1_ref[...]
        else:
            weights = jnp.concatenate(
                [
                    w1_ref[: wide * channels, b * (group1 + 2) * cin : b * (group1 + 2) * cin + span]
                    for b in range(3)
                ],
                axis=1,
            )
        source = jnp.concatenate(
            [x_ref[b, start * cin : start * cin + span, :] for b in range(3)], axis=0
        )
        result = jnp.maximum(jnp.dot(weights, source, preferred_element_type=F32), 0.0)
        for i in range(wide):
            piece = result[i * channels : (i + 1) * channels]
            if start + i == 0:
                piece = jnp.where(place == 0, 0.0, piece)
            if start + i == band + 1:
                piece = jnp.where(place == tiles - 1, 0.0, piece)
            parts = shifted(piece)
            at = (start + i) * channels
            for b in range(3):
                h_ref[b, at : at + channels, :] = parts[b].astype(BF16)
        start += wide
    head = head_ref[...]
    head = jnp.concatenate([head, head], axis=1)
    span = (group2 + 2) * channels
    logits = []
    for start in range(0, band, group2):
        at = start * channels
        pieces = []
        for lane in range(0, rows, chunk):
            source = jnp.concatenate(
                [h_ref[b, at : at + span, lane : lane + chunk] for b in range(3)], axis=0
            )
            deep = jnp.maximum(jnp.dot(w2_ref[...], source, preferred_element_type=F32), 0.0)
            pieces.append(
                jnp.concatenate(
                    [
                        jnp.sum(
                            deep[i * channels : (i + 1) * channels] * head, axis=0, keepdims=True
                        )
                        for i in range(group2)
                    ],
                    axis=0,
                )
            )
        logits.append(jnp.concatenate(pieces, axis=1))
    logits = jnp.concatenate(logits, axis=0)
    soft = jnp.maximum(logits, 0.0) + jnp.log1p(jnp.exp(-jnp.abs(logits)))
    rounded = soft.astype(BF16)
    for k in range(tiles):
        runoff_ref[k, 0] = rounded[:, k * height : (k + 1) * height]
    kept = rounded.astype(F32)
    for c in range(band):
        s_ref[c, pl.ds(step, 1), :] = kept[c : c + 1]

    @pl.when(step == pl.num_programs(0) - 1)
    def _():
        width = band * tiles
        depth = s_ref.shape[1]
        steps = s_ref[...].astype(BF16)
        sums = []
        for k in range(tiles):
            left, right = [], []
            own = gathered_ref[k, pl.ds(place * band, band), :].astype(jnp.int32)
            for c in range(band):
                left.append(steps[c, :, k * height : (k + 1) * height])
                right.append(
                    jnp.where(iota((count, height), 0) == own[c : c + 1], 1.0, 0.0).astype(BF16)
                )
            sums.append(
                lax.dot_general(
                    jnp.concatenate(left, axis=1),
                    jnp.concatenate(right, axis=1),
                    (((1,), (1,)), ((), ())),
                    preferred_element_type=F32,
                )
            )
        local = jnp.concatenate(sums, axis=1)
        local = jnp.where(iota(local.shape, 0) < pl.num_programs(0), local, 0.0)
        passed = route_matrix(gathered_ref, width, count)
        flow_ref[...] = jnp.dot(
            local, passed, precision=lax.Precision.HIGHEST, preferred_element_type=F32
        )


def banded(weight, group):
    cin, cout = weight.shape[2:]
    flat = jnp.transpose(weight, (3, 1, 0, 2))
    stacked = jnp.stack(
        [jnp.pad(flat, ((0, 0), (0, 0), (j, group - 1 - j), (0, 0))) for j in range(group)]
    )
    return stacked.reshape(group * cout, 3 * (group + 2) * cin)


def local(
    forcing,
    first_weight,
    second_weight,
    head_weight,
    flow_codes,
    outlet_cells,
    receivers,
    inlet_cells,
    levels,
):
    tiles = lax.axis_size("tile")
    step_count, band, cin, rows = forcing.shape
    width, height = flow_codes.shape
    count = outlet_cells.shape[1]
    channels = first_weight.shape[3]
    group1, group2 = 3, min(4, band)

    up = [(i, i + 1) for i in range(tiles - 1)]
    down = [(j, i) for i, j in up]
    before = lax.ppermute(lax.slice_in_dim(forcing, band - 2, band, axis=1), "tile", up)
    after = lax.ppermute(lax.slice_in_dim(forcing, 0, 2, axis=1), "tile", down)

    packed = pl.pallas_call(
        drain_kernel,
        out_shape=jax.ShapeDtypeStruct((width + count, height), F32),
        in_specs=[pl.BlockSpec(memory_space=pltpu.VMEM)] * 4
        + [pl.BlockSpec(memory_space=pltpu.SMEM)],
        out_specs=pl.BlockSpec(memory_space=pltpu.VMEM),
    )(flow_codes, outlet_cells, receivers, inlet_cells, levels)
    gathered = lax.all_to_all(
        jnp.broadcast_to(packed[None], (tiles,) + packed.shape), "tile", 0, 0, tiled=True
    )

    w1 = banded(first_weight, group1)
    w2 = banded(second_weight, group2)
    head = jnp.broadcast_to(head_weight.astype(F32)[:, None], (channels, 128))

    whole = lambda value: pl.BlockSpec(value.shape, lambda t: (0,) * value.ndim)
    per_step = lambda value: pl.BlockSpec((1,) + value.shape[1:], lambda t: (t, 0, 0, 0))
    padded_steps = -(-step_count // 16) * 16
    blocks, flows = pl.pallas_call(
        partial(conv_kernel, count, group1, group2),
        grid=(step_count,),
        in_specs=[
            per_step(before),
            per_step(forcing),
            per_step(after),
            whole(w1),
            whole(w2),
            whole(head),
            whole(gathered),
        ],
        out_shape=(
            jax.ShapeDtypeStruct((tiles, step_count, band, height), BF16),
            jax.ShapeDtypeStruct((padded_steps, tiles * count), F32),
        ),
        out_specs=(
            pl.BlockSpec((tiles, 1, band, height), lambda t: (0, t, 0, 0)),
            pl.BlockSpec((padded_steps, tiles * count), lambda t: (0, 0)),
        ),
        scratch_shapes=[
            pltpu.VMEM((3, (band + 4) * cin, rows), BF16),
            pltpu.VMEM((3, (band + 2) * channels, rows), BF16),
            pltpu.VMEM((band, padded_steps, rows), F32),
        ],
        compiler_params=pltpu.CompilerParams(vmem_limit_bytes=VMEM_BYTES),
    )(before, forcing, after, w1, w2, head, gathered)

    received = lax.all_to_all(blocks, "tile", 0, 0, tiled=True)
    runoff = jnp.transpose(received, (1, 0, 2, 3)).reshape(step_count, tiles * band, height)
    shares = flows[:step_count].reshape(step_count, tiles, count)
    shares = jnp.transpose(shares, (1, 2, 0))
    arrived = lax.all_to_all(shares, "tile", 0, 0, tiled=True)
    discharge = (jnp.sum(arrived, axis=0) * (count / (width * height)))[None]
    return (runoff, discharge)


def solution(mesh):
    placed = (
        P("tm", "tile", "grp", None),
        P(),
        P(),
        P(),
        P("grp", "tile"),
        P("tile", "grp"),
        P("tile", "grp"),
        P("tile", "grp"),
        P(("grp", "tile")),
    )
    return jax.shard_map(
        local,
        mesh=mesh,
        in_specs=placed,
        out_specs=(P("tm", "grp", "tile"), P("tile", "grp", "tm")),
        check_vma=False,
    )
```

time: 781 us -> 105 us (0.13)
  local copies, waits for them, and re-layouts: 397 us -> 11.9 us
  blocking collectives: 214 us -> 13 us
  matrix products: 129 us -> 0 us
  Pallas kernels: 0 us -> 33.3 us
  waiting for transfers between devices: 0.01 us -> 25.9 us
  other arithmetic: 17.5 us -> 1.05 us
    gather x9 -> x0, local copies, waits for them, and re-layouts: 366 us -> none  [the longest x8 364 us: drain_roots(): moved = moved[moved]]
    all_gather x7 -> x0, blocking collectives: 214 us -> none  [local(): everyone = lax.all_gather(sent_flow, 'tile', axis=0, tiled=True)]
    dot_general x224 -> x0, matrix products: 129 us -> none  [the longest x216 127 us: tap_sum(): jnp.einsum('wir,io->wor', window_cut, weights[column_tap, row_tap], prefe...]
    pallas_call x0 -> x2, Pallas kernels: none -> 33.3 us  [the longest x1 31 us: local(): pl.pallas_call(partial(conv_kernel, count, group1, group2), grid=(step_co...]
    all_to_all x2, waiting for transfers between devices: 0.01 us -> 25.9 us  [the longest x1 20.1 us: local(): lax.all_to_all(jnp.broadcast_to(packed[None], (tiles,) + packed.shape), '...]
    all_to_all x0 -> x1, blocking collectives: none -> 13 us  [local(): arrived = lax.all_to_all(shares, 'tile', 0, 0, tiled=True)]
    squeeze x12 -> x0, local copies, waits for them, and re-layouts: 12.6 us -> none  [local(): lax.map(partial(conv_layers, first_weight, second_weight, head_weight, ke...]
    unnamed x33 -> x10, local copies, waits for them, and re-layouts: 11.4 us -> 0.19 us
  transfers between devices with their start and end apart: 4 -> 4, of which waited for: 0 -> 2; matrix products, arithmetic and copies ran while one was open for 68% -> 7% of each run, Pallas kernels for 0% -> 2%
where the time goes in v1:
time: 105 us; the launch traced here: 104 us
  Pallas kernels  33.3 us (32%)
  waiting for transfers between devices  25.9 us (25%)
  starting transfers between devices  17.5 us (17%)
  blocking collectives  13 us (12%)
  local copies, waits for them, and re-layouts  11.9 us (11%)
  between operations  1.39 us (1%)
  other arithmetic  1.05 us (1%)
    pallas_call x1, Pallas kernels, local(): pl.pallas_call(partial(conv_kernel, count, group1, group2), grid=(step_co...  31 us
    all_to_all x1, waiting for transfers between devices, local(): lax.all_to_all(jnp.broadcast_to(packed[None], (tiles,) + packed.shape), '...  20.1 us
    all_to_all x1, blocking collectives, local(): arrived = lax.all_to_all(shares, 'tile', 0, 0, tiled=True)  13 us
    all_to_all x1, starting transfers between devices, local(): lax.all_to_all(jnp.broadcast_to(packed[None], (tiles,) + packed.shape), '...  6.99 us
    ppermute x1, starting transfers between devices, local(): lax.ppermute(lax.slice_in_dim(forcing, band - 2, band, axis=1), 'tile', up)  5.89 us
    all_to_all x1, waiting for transfers between devices, local(): received = lax.all_to_all(blocks, 'tile', 0, 0, tiled=True)  5.81 us
    reshape x4, local copies, waits for them, and re-layouts, banded(): return stacked.reshape(group * cout, 3 * (group + 2) * cin)  3.6 us
    all_to_all x1, starting transfers between devices, local(): received = lax.all_to_all(blocks, 'tile', 0, 0, tiled=True)  3.39 us
  transfers between devices with their start and end apart: 4, of which 2 were waited for; matrix products, arithmetic and copies ran while one was open for 7% of the time, Pallas kernels for 2%

profile of v1, /device:TPU:0, one launch (start us, length us, event | category | flops | bytes accessed | tf_op | source)
XLA Modules:
  0.0 104.1 jit_solution(2824015078419438074)
XLA Ops:
  0.6 2.7 %fusion = (bf16[12,2,16,1024]{3,2,1,0:T(8,128)(2,1)}, bf16[12,2,16,1024]{3,2,1,0:T(8,128)(2,1)}) fusion(bf16[12,8,16,1024]{3,2,1,0:T(8,128)(2,1)} %forcing_ref.1), kind=kLoop, calls=%fused_computation.12 | loop fusion | bytes 3145728 | tf_op jit(solution)/shard_map/slice | solution.py:254
  3.4 5.9 %collective-permute-start = (bf16[12,2,16,1024]{3,2,1,0:T(8,128)(2,1)}, bf16[12,2,16,1024]{3,2,1,0:T(8,128)(2,1)}, u32[]{:S(2)}, u32[]{:S(2)}) collective-permute-start(bf16[12,2,16,1024]{3,2,1,0:T(8,128)(2,1)} %get-tuple-element.7), channel_id=1, source_target_pairs={{0,2},{2,4},{4,6},{6,8},{8,10},{10,12},{12,14},{1,3},{3,5},{5,7},{... | collective-permute-start | bytes 2359304 | tf_op jit(solution)/shard_map/ppermute | solution.py:253
  9.3 1.3 %collective-permute-start.1 = (bf16[12,2,16,1024]{3,2,1,0:T(8,128)(2,1)}, bf16[12,2,16,1024]{3,2,1,0:T(8,128)(2,1)}, u32[]{:S(2)}, u32[]{:S(2)}) collective-permute-start(bf16[12,2,16,1024]{3,2,1,0:T(8,128)(2,1)} %get-tuple-element.6), channel_id=1, source_target_pairs={{2,0},{4,2},{6,4},{8,6},{10,8},{12,10},{14,12},{3,1},{5,3},{7,5},{... | collective-permute-start | bytes 2359304 | tf_op jit(solution)/shard_map/ppermute | solution.py:254
  11.2 2.2 %shard_map.104 = f32[96,128]{1,0:T(8,128)} custom-call(s32[64,128]{1,0:T(8,128)} %codes_ref.1, s32[1,32]{1,0:T(1,128)} %outlets_ref.1, s32[1,32]{1,0:T(1,128)} %receivers_ref.1, s32[1,32]{1,0:T(1,128)} %inlets_ref.1, s32[1]{0:T(128)S(6)} %copy.31.levels_ref), custom_call_target="tpu_custom_call" | custom-call | tf_op jit(solution)/shard_map/pallas_call | solution.py:256
  13.4 1.6 %broadcast_in_dim.5 = f32[8,96,128]{2,1,0:T(8,128)} broadcast(f32[96,128]{1,0:T(8,128)} %shard_map.104), dimensions={1,2} | broadcast | bytes 442368 | tf_op jit(solution)/shard_map/broadcast_in_dim | solution.py:264
  15.0 7.0 %all-to-all-start = ((f32[8,96,128]{2,1,0:T(8,128)}), f32[8,96,128]{2,1,0:T(8,128)S(1)}, u32[]{:S(2)}, u32[]{:S(2)}) async-start(f32[8,96,128]{2,1,0:T(8,128)} %broadcast_in_dim.5), calls=%async_computation | async-start | bytes 786432 | tf_op jit(solution)/shard_map/all_to_all | solution.py:263
  22.0 0.0 copy-done.1
  22.0 0.3 pad_bitcast_fusion.3
  22.3 0.3 pad_maximum_fusion
  22.6 1.0 copy.24
  23.6 0.0 copy-start.2
  23.6 1.7 %reshape.31.w2_ref = bf16[256,1152]{1,0:T(8,128)(2,1)} reshape(bf16[4,64,3,6,64]{4,3,2,1,0:T(8,128)(2,1)S(1)} %copy.24) | data formatting | bytes 1179648 | tf_op jit(solution)/shard_map/reshape | solution.py:230
  25.4 0.1 copy.18
  25.5 0.2 reshape.27
  25.7 0.7 copy.20.w1_ref
  26.4 20.1 %all-to-all-done.gathered_ref = f32[8,96,128]{2,1,0:T(8,128)S(1)} async-done(((f32[8,96,128]{2,1,0:T(8,128)}), f32[8,96,128]{2,1,0:T(8,128)S(1)}, u32[]{:S(2)}, u32[]{:S(2)}) %all-to-all-start) | async-done | bytes 393248 | tf_op jit(solution)/shard_map/all_to_all | solution.py:263
  46.5 0.0 collective-permute-done.before_ref
  46.5 0.0 collective-permute-done.1.after_ref
  46.5 0.0 copy-done.3
  46.6 0.7 broadcast_in_dim.4.head_ref
  47.3 0.0 copy-done
  47.3 31.0 %shard_map.105 = (bf16[8,12,8,128]{3,2,1,0:T(8,128)(2,1)}, f32[16,256]{1,0:T(8,128)}) custom-call(bf16[12,2,16,1024]{3,2,1,0:T(8,128)(2,1)} %collective-permute-done.before_ref, bf16[12,8,16,1024]{3,2,1,0:T(8,128)(2,1)} %forcing_ref.1, bf16[12,2,16,1024]{3,2,1,0:T(8,128)(2,1)} %collective-permute-done.1.after_ref, bf16[192,240]{1,0:T(8,128)(2,1)} %copy.20.w1_ref, ...), custom_call_target="tpu_custom_call" | custom-call | tf_op jit(solution)/shard_map/pallas_call | solution.py:274
  78.4 0.8 reshape.30
  79.2 0.1 reshape.32
  79.3 13.0 %all_to_all.15 = f32[8,1,384]{2,1,0:T(1,128)S(1)} all-to-all(f32[8,1,384]{2,1,0:T(1,128)S(1)} %reshape.32), channel_id=1, replica_groups=mesh['grp'=2,'tile'=8,'tm'=2] {'tile'}, dimensions={0} | all-to-all | bytes 24576 | tf_op jit(solution)/shard_map/all_to_all | solution.py:306
  92.2 3.4 %all-to-all-start.1 = ((bf16[8,12,8,128]{3,2,1,0:T(8,128)(2,1)}), bf16[8,12,8,128]{3,2,1,0:T(8,128)(2,1)S(1)}, u32[]{:S(2)}, u32[]{:S(2)}) async-start(bf16[8,12,8,128]{3,2,1,0:T(8,128)(2,1)} %get-tuple-element.4), calls=%async_computation.1 | async-start | bytes 393216 | tf_op jit(solution)/shard_map/all_to_all | solution.py:302
  95.6 0.5 broadcast.25
  96.2 0.7 reduce
  96.8 0.1 reshape.33
  97.0 0.6 mul.18
  97.6 5.8 %all-to-all-done.1 = bf16[8,12,8,128]{3,2,1,0:T(8,128)(2,1)S(1)} async-done(((bf16[8,12,8,128]{3,2,1,0:T(8,128)(2,1)}), bf16[8,12,8,128]{3,2,1,0:T(8,128)(2,1)S(1)}, u32[]{:S(2)}, u32[]{:S(2)}) %all-to-all-start.1) | async-done | bytes 196640 | tf_op jit(solution)/shard_map/all_to_all | solution.py:302
  103.4 0.7 copy_bitcast_fusion
  (9 shorter events, 0.1 us)
Async XLA Ops:
  3.4 18.6 %copy-start.1 = (bf16[3,3,64,64]{3,2,1,0:T(8,128)(2,1)S(1)}, bf16[3,3,64,64]{3,2,1,0:T(8,128)(2,1)}, u32[]{:S(2)}) copy-start(bf16[3,3,64,64]{3,2,1,0:T(8,128)(2,1)} %param.11) | copy-start | bytes 221188
  3.4 43.2 %collective-permute-start = (bf16[12,2,16,1024]{3,2,1,0:T(8,128)(2,1)}, bf16[12,2,16,1024]{3,2,1,0:T(8,128)(2,1)}, u32[]{:S(2)}, u32[]{:S(2)}) collective-permute-start(bf16[12,2,16,1024]{3,2,1,0:T(8,128)(2,1)} %get-tuple-element.7), channel_id=1, source_target_pairs={{0,2},{2,4},{4,6},{6,8},{8,10},{10,12},{12,14},{1,3},{3,5},{5,7},{... | collective-permute-start | bytes 2359304 | tf_op jit(solution)/shard_map/ppermute | solution.py:253
  9.3 37.3 %collective-permute-start.1 = (bf16[12,2,16,1024]{3,2,1,0:T(8,128)(2,1)}, bf16[12,2,16,1024]{3,2,1,0:T(8,128)(2,1)}, u32[]{:S(2)}, u32[]{:S(2)}) collective-permute-start(bf16[12,2,16,1024]{3,2,1,0:T(8,128)(2,1)} %get-tuple-element.6), channel_id=1, source_target_pairs={{2,0},{4,2},{6,4},{8,6},{10,8},{12,10},{14,12},{3,1},{5,3},{7,5},{... | collective-permute-start | bytes 2359304 | tf_op jit(solution)/shard_map/ppermute | solution.py:254
  15.0 31.5 %all-to-all-start = ((f32[8,96,128]{2,1,0:T(8,128)}), f32[8,96,128]{2,1,0:T(8,128)S(1)}, u32[]{:S(2)}, u32[]{:S(2)}) async-start(f32[8,96,128]{2,1,0:T(8,128)} %broadcast_in_dim.5), calls=%async_computation | async-start | bytes 786432 | tf_op jit(solution)/shard_map/all_to_all | solution.py:263
  23.6 1.7 %copy-start.2 = (bf16[3,3,16,64]{3,2,1,0:T(8,128)(2,1)S(1)}, bf16[3,3,16,64]{3,2,1,0:T(8,128)(2,1)}, u32[]{:S(2)}) copy-start(bf16[3,3,16,64]{3,2,1,0:T(8,128)(2,1)} %param.10) | copy-start | bytes 55300
  25.3 21.3 %copy-start.3 = (bf16[64]{0:T(256)(128)(2,1)S(1)}, bf16[64]{0:T(256)(128)(2,1)}, u32[]{:S(2)}) copy-start(bf16[64]{0:T(256)(128)(2,1)} %param.12) | copy-start | bytes 388
  46.5 0.8 copy-start
  92.2 11.1 %all-to-all-start.1 = ((bf16[8,12,8,128]{3,2,1,0:T(8,128)(2,1)}), bf16[8,12,8,128]{3,2,1,0:T(8,128)(2,1)S(1)}, u32[]{:S(2)}, u32[]{:S(2)}) async-start(bf16[8,12,8,128]{3,2,1,0:T(8,128)(2,1)} %get-tuple-element.4), calls=%async_computation.1 | async-start | bytes 393216 | tf_op jit(solution)/shard_map/all_to_all | solution.py:302

commit v2 on v1

--- a/solution.py
+++ b/solution.py
@@ -98,8 +98,29 @@
     return passed
 
 
-def conv_kernel(
-    count,
+def lay_out(weight_ref, out_ref, group):
+    cin, cout = weight_ref.shape[2:]
+    same = jnp.where(iota((cout, cout), 0) == iota((cout, cout), 1), 1.0, 0.0).astype(BF16)
+    for j in range(group):
+        parts = []
+        for b in range(3):
+            if j > 0:
+                parts.append(jnp.zeros((j * cin, cout), BF16))
+            parts += [weight_ref[a, b] for a in range(3)]
+            if j < group - 1:
+                parts.append(jnp.zeros(((group - 1 - j) * cin, cout), BF16))
+        out_ref[j * cout : (j + 1) * cout, :] = lax.dot_general(
+            same,
+            jnp.concatenate(parts, axis=0),
+            (((1,), (1,)), ((), ())),
+            preferred_element_type=F32,
+        ).astype(BF16)
+
+
+def one_step(
+    step,
+    place,
+    tiles,
     group1,
     group2,
     before_ref,
@@ -108,24 +129,16 @@
     w1_ref,
     w2_ref,
     head_ref,
-    gathered_ref,
-    runoff_ref,
-    flow_ref,
     x_ref,
     h_ref,
-    s_ref,
 ):
-    step = pl.program_id(0)
-    place = lax.axis_index("tile")
-    tiles = runoff_ref.shape[0]
     _, band, cin, rows = forcing_ref.shape
-    height = runoff_ref.shape[3]
     channels = head_ref.shape[0]
     chunk = 256
     first = 0
     for ref in (before_ref, forcing_ref, after_ref):
         depth = ref.shape[1] * cin
-        parts = shifted(ref[0].reshape(depth, rows).astype(F32))
+        parts = shifted(ref[step].reshape(depth, rows).astype(F32))
         for b in range(3):
             x_ref[b, first : first + depth, :] = parts[b].astype(BF16)
         first += depth
@@ -158,8 +171,7 @@
             for b in range(3):
                 h_ref[b, at : at + channels, :] = parts[b].astype(BF16)
         start += wide
-    head = head_ref[...]
-    head = jnp.concatenate([head, head], axis=1)
+    head = jnp.concatenate([head_ref[...]] * 2, axis=1)
     span = (group2 + 2) * channels
     logits = []
     for start in range(0, band, group2):
@@ -184,50 +196,238 @@
         logits.append(jnp.concatenate(pieces, axis=1))
     logits = jnp.concatenate(logits, axis=0)
     soft = jnp.maximum(logits, 0.0) + jnp.log1p(jnp.exp(-jnp.abs(logits)))
-    rounded = soft.astype(BF16)
+    return soft.astype(BF16)
+
+
+def band_sums(place, count, gathered_ref, s_ref):
+    tiles, _, height = gathered_ref.shape
+    band = s_ref.shape[0]
+    steps = s_ref[...].astype(BF16)
+    sums = []
     for k in range(tiles):
-        runoff_ref[k, 0] = rounded[:, k * height : (k + 1) * height]
-    kept = rounded.astype(F32)
-    for c in range(band):
-        s_ref[c, pl.ds(step, 1), :] = kept[c : c + 1]
-
-    @pl.when(step == pl.num_programs(0) - 1)
+        left, right = [], []
+        own = gathered_ref[k, pl.ds(place * band, band), :].astype(jnp.int32)
+        for c in range(band):
+            left.append(steps[c, :, k * height : (k + 1) * height])
+            right.append(
+                jnp.where(iota((count, height), 0) == own[c : c + 1], 1.0, 0.0).astype(BF16)
+            )
+        sums.append(
+            lax.dot_general(
+                jnp.concatenate(left, axis=1),
+                jnp.concatenate(right, axis=1),
+                (((1,), (1,)), ((), ())),
+                preferred_element_type=F32,
+            )
+        )
+    return jnp.concatenate(sums, axis=1)
+
+
+def main_kernel(
+    count,
+    group1,
+    group2,
+    forcing_ref,
+    first_ref,
+    second_ref,
+    headrow_ref,
+    packed_ref,
+    runoff_ref,
+    flow_ref,
+    before_ref,
+    after_ref,
+    gathered_ref,
+    w1_ref,
+    w2_ref,
+    head_ref,
+    x_ref,
+    h_ref,
+    s_ref,
+    out_ref,
+    share_ref,
+    landed_ref,
+    halo_send,
+    halo_recv,
+    table_send,
+    table_recv,
+    runoff_send,
+    runoff_recv,
+    share_send,
+    share_recv,
+):
+    place = lax.axis_index("tile")
+    tiles, step_count, band, height = runoff_ref.shape
+    batches = runoff_send.shape[0]
+    per = step_count // batches
+
+    def each_peer(act):
+        def turn(d, carry):
+            act(d, lax.rem(place + d, tiles), lax.rem(place + tiles - d, tiles))
+            return carry
+
+        lax.fori_loop(1, tiles, turn, 0)
+
+    def remote(source, landing, send, recv, peer):
+        return pltpu.make_async_remote_copy(
+            src_ref=source,
+            dst_ref=landing,
+            send_sem=send,
+            recv_sem=recv,
+            device_id={"tile": peer},
+            device_id_type=pl.DeviceIdType.MESH,
+        )
+
+    def halo_up(t):
+        return remote(
+            forcing_ref.at[t, pl.ds(band - 2, 2)],
+            before_ref.at[t],
+            halo_send.at[0, t],
+            halo_recv.at[0, t],
+            place + 1,
+        )
+
+    def halo_down(t):
+        return remote(
+            forcing_ref.at[t, pl.ds(0, 2)],
+            after_ref.at[t],
+            halo_send.at[1, t],
+            halo_recv.at[1, t],
+            place - 1,
+        )
+
+    def table(d, peer, slot):
+        return remote(
+            packed_ref, gathered_ref.at[slot], table_send.at[d], table_recv.at[d], peer
+        )
+
+    def runoff_part(g, d, peer, slot):
+        return remote(
+            out_ref.at[peer, pl.ds(g * per, per)],
+            runoff_ref.at[slot, pl.ds(g * per, per)],
+            runoff_send.at[g, d],
+            runoff_recv.at[g, d],
+            peer,
+        )
+
+    def share(d, peer, slot):
+        return remote(
+            share_ref.at[peer], landed_ref.at[slot], share_send.at[d], share_recv.at[d], peer
+        )
+
+    barrier = pltpu.get_barrier_semaphore()
+    each_peer(
+        lambda d, peer, source: pl.semaphore_signal(
+            barrier, inc=1, device_id={"tile": peer}, device_id_type=pl.DeviceIdType.MESH
+        )
+    )
+    pl.semaphore_wait(barrier, tiles - 1)
+
+    def start_halos(t, carry):
+        @pl.when(place < tiles - 1)
+        def _():
+            halo_up(t).start()
+
+        @pl.when(place > 0)
+        def _():
+            halo_down(t).start()
+
+        return carry
+
+    lax.fori_loop(0, step_count, start_halos, 0)
+    each_peer(lambda d, peer, source: table(d, peer, place).start())
+
+    @pl.when(place == 0)
     def _():
-        width = band * tiles
-        depth = s_ref.shape[1]
-        steps = s_ref[...].astype(BF16)
-        sums = []
-        for k in range(tiles):
-            left, right = [], []
-            own = gathered_ref[k, pl.ds(place * band, band), :].astype(jnp.int32)
+        before_ref[...] = jnp.zeros_like(before_ref)
+
+    @pl.when(place == tiles - 1)
+    def _():
+        after_ref[...] = jnp.zeros_like(after_ref)
+
+    gathered_ref[place] = packed_ref[...]
+    s_ref[...] = jnp.zeros_like(s_ref)
+    lay_out(first_ref, w1_ref, group1)
+    lay_out(second_ref, w2_ref, group2)
+    channels = head_ref.shape[0]
+    head_ref[...] = jnp.broadcast_to(as_column(headrow_ref[...], channels), head_ref.shape)
+
+    def batch(g, carry):
+        def turn(i, inner):
+            t = g * per + i
+
+            @pl.when(place > 0)
+            def _():
+                halo_up(t).wait_recv()
+
+            @pl.when(place < tiles - 1)
+            def _():
+                halo_down(t).wait_recv()
+
+            rounded = one_step(
+                t,
+                place,
+                tiles,
+                group1,
+                group2,
+                before_ref,
+                forcing_ref,
+                after_ref,
+                w1_ref,
+                w2_ref,
+                head_ref,
+                x_ref,
+                h_ref,
+            )
+            for k in range(tiles):
+                out_ref[k, t] = rounded[:, k * height : (k + 1) * height]
+            kept = rounded.astype(F32)
             for c in range(band):
-                left.append(steps[c, :, k * height : (k + 1) * height])
-                right.append(
-                    jnp.where(iota((count, height), 0) == own[c : c + 1], 1.0, 0.0).astype(BF16)
-                )
-            sums.append(
-                lax.dot_general(
-                    jnp.concatenate(left, axis=1),
-                    jnp.concatenate(right, axis=1),
-                    (((1,), (1,)), ((), ())),
-                    preferred_element_type=F32,
-                )
-            )
-        local = jnp.concatenate(sums, axis=1)
-        local = jnp.where(iota(local.shape, 0) < pl.num_programs(0), local, 0.0)
-        passed = route_matrix(gathered_ref, width, count)
-        flow_ref[...] = jnp.dot(
-            local, passed, precision=lax.Precision.HIGHEST, preferred_element_type=F32
-        )
-
-
-def banded(weight, group):
-    cin, cout = weight.shape[2:]
-    flat = jnp.transpose(weight, (3, 1, 0, 2))
-    stacked = jnp.stack(
-        [jnp.pad(flat, ((0, 0), (0, 0), (j, group - 1 - j), (0, 0))) for j in range(group)]
-    )
-    return stacked.reshape(group * cout, 3 * (group + 2) * cin)
+                s_ref[c, pl.ds(t, 1), :] = kept[c : c + 1]
+            return inner
+
+        lax.fori_loop(0, per, turn, 0)
+        each_peer(lambda d, peer, source: runoff_part(g, d, peer, place).start())
+        return carry
+
+    lax.fori_loop(0, batches, batch, 0)
+    runoff_ref[place] = out_ref[place]
+
+    each_peer(lambda d, peer, source: table(d, peer, source).wait_recv())
+    local_sums = band_sums(place, count, gathered_ref, s_ref)
+    passed = route_matrix(gathered_ref, band * tiles, count)
+    flows = jnp.dot(
+        local_sums, passed, precision=lax.Precision.HIGHEST, preferred_element_type=F32
+    )
+    filler = jnp.zeros((flows.shape[0], share_ref.shape[2] - count), F32)
+    for k in range(tiles):
+        share_ref[k] = jnp.concatenate([flows[:, k * count : (k + 1) * count], filler], axis=1)
+    each_peer(lambda d, peer, source: share(d, peer, place).start())
+    landed_ref[place] = share_ref[place]
+    each_peer(lambda d, peer, source: share(d, peer, source).wait_recv())
+    scale = count / (band * tiles * height)
+    flow_ref[...] = jnp.sum(landed_ref[...], axis=0) * scale
+
+    def finish(g, carry):
+        each_peer(lambda d, peer, source: runoff_part(g, d, peer, source).wait_recv())
+        each_peer(lambda d, peer, source: runoff_part(g, d, peer, place).wait_send())
+        return carry
+
+    lax.fori_loop(0, batches, finish, 0)
+    each_peer(lambda d, peer, source: share(d, peer, place).wait_send())
+    each_peer(lambda d, peer, source: table(d, peer, place).wait_send())
+
+    def end_halos(t, carry):
+        @pl.when(place < tiles - 1)
+        def _():
+            halo_up(t).wait_send()
+
+        @pl.when(place > 0)
+        def _():
+            halo_down(t).wait_send()
+
+        return carry
+
+    lax.fori_loop(0, step_count, end_halos, 0)
 
 
 def local(
@@ -248,11 +448,6 @@
     channels = first_weight.shape[3]
     group1, group2 = 3, min(4, band)
 
-    up = [(i, i + 1) for i in range(tiles - 1)]
-    down = [(j, i) for i, j in up]
-    before = lax.ppermute(lax.slice_in_dim(forcing, band - 2, band, axis=1), "tile", up)
-    after = lax.ppermute(lax.slice_in_dim(forcing, 0, 2, axis=1), "tile", down)
-
     packed = pl.pallas_call(
         drain_kernel,
         out_shape=jax.ShapeDtypeStruct((width + count, height), F32),
@@ -260,51 +455,47 @@
         + [pl.BlockSpec(memory_space=pltpu.SMEM)],
         out_specs=pl.BlockSpec(memory_space=pltpu.VMEM),
     )(flow_codes, outlet_cells, receivers, inlet_cells, levels)
-    gathered = lax.all_to_all(
-        jnp.broadcast_to(packed[None], (tiles,) + packed.shape), "tile", 0, 0, tiled=True
-    )
-
-    w1 = banded(first_weight, group1)
-    w2 = banded(second_weight, group2)
-    head = jnp.broadcast_to(head_weight.astype(F32)[:, None], (channels, 128))
-
-    whole = lambda value: pl.BlockSpec(value.shape, lambda t: (0,) * value.ndim)
-    per_step = lambda value: pl.BlockSpec((1,) + value.shape[1:], lambda t: (t, 0, 0, 0))
     padded_steps = -(-step_count // 16) * 16
+    batches = step_count // 3 if step_count % 3 == 0 else step_count
+    dma = pltpu.SemaphoreType.DMA
+    vmem = pl.BlockSpec(memory_space=pltpu.VMEM)
     blocks, flows = pl.pallas_call(
-        partial(conv_kernel, count, group1, group2),
-        grid=(step_count,),
-        in_specs=[
-            per_step(before),
-            per_step(forcing),
-            per_step(after),
-            whole(w1),
-            whole(w2),
-            whole(head),
-            whole(gathered),
-        ],
+        partial(main_kernel, count, group1, group2),
+        in_specs=[vmem] * 5,
         out_shape=(
             jax.ShapeDtypeStruct((tiles, step_count, band, height), BF16),
-            jax.ShapeDtypeStruct((padded_steps, tiles * count), F32),
+            jax.ShapeDtypeStruct((padded_steps, 128), F32),
         ),
-        out_specs=(
-            pl.BlockSpec((tiles, 1, band, height), lambda t: (0, t, 0, 0)),
-            pl.BlockSpec((padded_steps, tiles * count), lambda t: (0, 0)),
-        ),
+        out_specs=(vmem, vmem),
         scratch_shapes=[
+            pltpu.VMEM((step_count, 2, cin, rows), BF16),
+            pltpu.VMEM((step_count, 2, cin, rows), BF16),
+            pltpu.VMEM((tiles, width + count, height), F32),
+            pltpu.VMEM((group1 * channels, 3 * (group1 + 2) * cin), BF16),
+            pltpu.VMEM((group2 * channels, 3 * (group2 + 2) * channels), BF16),
+            pltpu.VMEM((channels, 128), F32),
             pltpu.VMEM((3, (band + 4) * cin, rows), BF16),
             pltpu.VMEM((3, (band + 2) * channels, rows), BF16),
             pltpu.VMEM((band, padded_steps, rows), F32),
+            pltpu.VMEM((tiles, step_count, band, height), BF16),
+            pltpu.VMEM((tiles, padded_steps, 128), F32),
+            pltpu.VMEM((tiles, padded_steps, 128), F32),
+            dma((2, step_count)),
+            dma((2, step_count)),
+            dma((tiles,)),
+            dma((tiles,)),
+            dma((batches, tiles)),
+            dma((batches, tiles)),
+            dma((tiles,)),
+            dma((tiles,)),
         ],
-        compiler_params=pltpu.CompilerParams(vmem_limit_bytes=VMEM_BYTES),
-    )(before, forcing, after, w1, w2, head, gathered)
-
-    received = lax.all_to_all(blocks, "tile", 0, 0, tiled=True)
-    runoff = jnp.transpose(received, (1, 0, 2, 3)).reshape(step_count, tiles * band, height)
-    shares = flows[:step_count].reshape(step_count, tiles, count)
-    shares = jnp.transpose(shares, (1, 2, 0))
-    arrived = lax.all_to_all(shares, "tile", 0, 0, tiled=True)
-    discharge = (jnp.sum(arrived, axis=0) * (count / (width * height)))[None]
+        compiler_params=pltpu.CompilerParams(
+            collective_id=0, has_side_effects=True, vmem_limit_bytes=VMEM_BYTES
+        ),
+    )(forcing, first_weight, second_weight, head_weight[None], packed)
+
+    runoff = jnp.transpose(blocks, (1, 0, 2, 3)).reshape(step_count, tiles * band, height)
+    discharge = flows[:step_count, :count].T[None]
     return (runoff, discharge)
 
 

time: 105 us -> 72.4 us (0.69)
  Pallas kernels: 33.3 us -> 67.9 us
  waiting for transfers between devices: 25.9 us -> 0 us
  starting transfers between devices: 17.5 us -> 0 us
  blocking collectives: 13 us -> 0 us
  local copies, waits for them, and re-layouts: 11.9 us -> 2.95 us
  other arithmetic: 1.05 us -> 0 us
    pallas_call x1, Pallas kernels: 31 us -> 65.7 us  [local(): pl.pallas_call(partial(main_kernel, count, group1, group2), in_specs=[vme...]
    all_to_all x2 -> x0, waiting for transfers between devices: 25.9 us -> none  [the longest x1 20.1 us: local(): lax.all_to_all(jnp.broadcast_to(packed[None], (tiles,) + packed.shape), '...]
    all_to_all x1 -> x0, blocking collectives: 13 us -> none  [local(): arrived = lax.all_to_all(shares, 'tile', 0, 0, tiled=True)]
    all_to_all x2 -> x0, starting transfers between devices: 10.4 us -> none  [the longest x1 6.99 us: local(): lax.all_to_all(jnp.broadcast_to(packed[None], (tiles,) + packed.shape), '...]
    ppermute x2 -> x0, starting transfers between devices: 7.17 us -> none  [the longest x1 5.89 us: local(): lax.ppermute(lax.slice_in_dim(forcing, band - 2, band, axis=1), 'tile', up)]
    reshape x7 -> x1, local copies, waits for them, and re-layouts: 5.13 us -> 1.65 us  [local(): jnp.transpose(blocks, (1, 0, 2, 3))]
    slice x1 -> x0, local copies, waits for them, and re-layouts: 2.75 us -> none  [local(): after = lax.ppermute(lax.slice_in_dim(forcing, 0, 2, axis=1), 'tile', down)]
    broadcast_in_dim x2 -> x1, local copies, waits for them, and re-layouts: 2.31 us -> 0.7 us  [local(): discharge = flows[:step_count, :count].T[None]]
  transfers between devices with their start and end apart: 4 -> 0, of which waited for: 2 -> 0; matrix products, arithmetic and copies ran while one was open for 7% -> 0% of each run, Pallas kernels for 2% -> 0%
where the time goes in v2:
time: 72.4 us; the launch traced here: 72.1 us
  Pallas kernels  67.9 us (94%)
  local copies, waits for them, and re-layouts  2.95 us (4%)
  between operations  1.29 us (2%)
    pallas_call x1, Pallas kernels, local(): pl.pallas_call(partial(main_kernel, count, group1, group2), in_specs=[vme...  65.7 us
    pallas_call x1, Pallas kernels, local(): pl.pallas_call(drain_kernel, out_shape=jax.ShapeDtypeStruct((width + coun...  2.25 us
    reshape x1, local copies, waits for them, and re-layouts, local(): jnp.transpose(blocks, (1, 0, 2, 3))  1.65 us

profile of v2, /device:TPU:0, one launch (start us, length us, event | category | flops | bytes accessed | tf_op | source)
XLA Modules:
  0.0 72.1 jit_solution(8523533365033217850)
XLA Ops:
  1.3 2.2 %shard_map.104.packed_ref = f32[96,128]{1,0:T(8,128)} custom-call(s32[64,128]{1,0:T(8,128)} %codes_ref.1, s32[1,32]{1,0:T(1,128)} %outlets_ref.1, s32[1,32]{1,0:T(1,128)} %receivers_ref.1, s32[1,32]{1,0:T(1,128)} %inlets_ref.1, s32[1]{0:T(128)S(6)} %copy.15.levels_ref), custom_call_target="tpu_custom_call" | custom-call | tf_op jit(solution)/shard_map/pallas_call | solution.py:451
  3.5 65.7 %shard_map.105 = (bf16[8,12,8,128]{3,2,1,0:T(8,128)(2,1)}, f32[16,128]{1,0:T(8,128)}) custom-call(bf16[12,8,16,1024]{3,2,1,0:T(8,128)(2,1)} %forcing_ref.1, bf16[3,3,16,64]{3,2,1,0:T(8,128)(2,1)} %first_ref.1, bf16[3,3,64,64]{3,2,1,0:T(8,128)(2,1)} %second_ref.1, bf16[1,64]{1,0:T(2,128)(2,1)} %bitcast.10, f32[96,128]{1,0:T(8,128)} %shard_map.104.packed_ref), custom_call_target="tpu_custom_call" | custom-call | tf_op jit(solution)/shard_map/pallas_call | solution.py:462
  69.2 1.7 %copy_bitcast_fusion = bf16[12,64,128]{2,1,0:T(8,128)(2,1)} fusion(bf16[8,12,8,128]{3,2,1,0:T(8,128)(2,1)} %get-tuple-element.4), kind=kLoop, calls=%fused_computation | loop fusion | bytes 393216 | tf_op jit(solution)/shard_map/reshape | solution.py:497
  70.8 0.7 slice_bitcast_fusion
  71.5 0.6 copy.13

commit v3 on v2

--- a/solution.py
+++ b/solution.py
@@ -11,6 +11,7 @@
 F32 = jnp.float32
 BF16 = jnp.bfloat16
 VMEM_BYTES = 56 * 1024 * 1024
+AHEAD = 3
 
 
 def iota(shape, dim):
@@ -52,12 +53,14 @@
     drained = jnp.take_along_axis(
         jnp.broadcast_to(nearest, shape), landing, axis=1, mode="promise_in_bounds"
     )
-    packed_ref[:width, :] = drained.astype(F32).T[:width]
+    packed_ref[:width, :] = drained.astype(F32).T[:width].astype(BF16)
     lane = iota((count, height), 1)
     table = jnp.where(lane == 0, as_column(receivers_ref[...], count), 0.0)
-    table = jnp.where(lane == 1, as_column(inlets_ref[...], count), table)
-    table = jnp.where(lane == 2, levels_ref[0].astype(F32), table)
-    packed_ref[width:, :] = table
+    inlets = jnp.maximum(as_column(inlets_ref[...], count).astype(jnp.int32), 0)
+    table = jnp.where(lane == 1, (inlets // height).astype(F32), table)
+    table = jnp.where(lane == 2, (inlets % height).astype(F32), table)
+    table = jnp.where(lane == 3, levels_ref[0].astype(F32), table)
+    packed_ref[width:, :] = table.astype(BF16)
 
 
 def shifted(value):
@@ -71,13 +74,12 @@
 def route_matrix(gathered_ref, width, count):
     tiles, depth, height = gathered_ref.shape
     everything = tiles * count
-    table = gathered_ref[:, width:, :].reshape(everything, height)
+    table = gathered_ref[:, width:, :].reshape(everything, height).astype(F32)
     receiver = table[:, 0:1].astype(jnp.int32)
-    inlet = table[:, 1:2].astype(jnp.int32)
-    sends = (receiver >= 0) & (table[:, 2:3] < LEVELS - 1.0)
-    inlet_column = jnp.maximum(inlet, 0) // height
-    inlet_row = jnp.maximum(inlet, 0) % height
-    drained = gathered_ref[:, :width, :].reshape(tiles * width, height).astype(BF16)
+    inlet_column = table[:, 1:2].astype(jnp.int32)
+    inlet_row = table[:, 2:3].astype(jnp.int32)
+    sends = (receiver >= 0) & (table[:, 3:4] < LEVELS - 1.0)
+    drained = gathered_ref[:, :width, :].reshape(tiles * width, height)
     picks = jnp.where(
         iota((everything, tiles * width), 1) == receiver * width + inlet_column, 1.0, 0.0
     ).astype(BF16)
@@ -199,14 +201,15 @@
     return soft.astype(BF16)
 
 
-def band_sums(place, count, gathered_ref, s_ref):
+def band_sums(place, count, gathered_ref, cells_ref, s_ref):
     tiles, _, height = gathered_ref.shape
     band = s_ref.shape[0]
     steps = s_ref[...].astype(BF16)
+    cells_ref[...] = gathered_ref[:, : cells_ref.shape[1], :].astype(F32)
     sums = []
     for k in range(tiles):
         left, right = [], []
-        own = gathered_ref[k, pl.ds(place * band, band), :].astype(jnp.int32)
+        own = cells_ref[k, pl.ds(place * band, band), :].astype(jnp.int32)
         for c in range(band):
             left.append(steps[c, :, k * height : (k + 1) * height])
             right.append(
@@ -237,6 +240,7 @@
     before_ref,
     after_ref,
     gathered_ref,
+    cells_ref,
     w1_ref,
     w2_ref,
     head_ref,
@@ -333,8 +337,7 @@
 
         return carry
 
-    lax.fori_loop(0, step_count, start_halos, 0)
-    each_peer(lambda d, peer, source: table(d, peer, place).start())
+    lax.fori_loop(0, AHEAD, start_halos, 0)
 
     @pl.when(place == 0)
     def _():
@@ -362,6 +365,10 @@
             @pl.when(place < tiles - 1)
             def _():
                 halo_down(t).wait_recv()
+
+            @pl.when(t + AHEAD < step_count)
+            def _():
+                start_halos(t + AHEAD, 0)
 
             rounded = one_step(
                 t,
@@ -387,13 +394,18 @@
 
         lax.fori_loop(0, per, turn, 0)
         each_peer(lambda d, peer, source: runoff_part(g, d, peer, place).start())
+
+        @pl.when(g == batches // 2 - 1)
+        def _():
+            each_peer(lambda d, peer, source: table(d, peer, place).start())
+
         return carry
 
     lax.fori_loop(0, batches, batch, 0)
     runoff_ref[place] = out_ref[place]
 
     each_peer(lambda d, peer, source: table(d, peer, source).wait_recv())
-    local_sums = band_sums(place, count, gathered_ref, s_ref)
+    local_sums = band_sums(place, count, gathered_ref, cells_ref, s_ref)
     passed = route_matrix(gathered_ref, band * tiles, count)
     flows = jnp.dot(
         local_sums, passed, precision=lax.Precision.HIGHEST, preferred_element_type=F32
@@ -450,7 +462,7 @@
 
     packed = pl.pallas_call(
         drain_kernel,
-        out_shape=jax.ShapeDtypeStruct((width + count, height), F32),
+        out_shape=jax.ShapeDtypeStruct((width + count, height), BF16),
         in_specs=[pl.BlockSpec(memory_space=pltpu.VMEM)] * 4
         + [pl.BlockSpec(memory_space=pltpu.SMEM)],
         out_specs=pl.BlockSpec(memory_space=pltpu.VMEM),
@@ -470,7 +482,8 @@
         scratch_shapes=[
             pltpu.VMEM((step_count, 2, cin, rows), BF16),
             pltpu.VMEM((step_count, 2, cin, rows), BF16),
-            pltpu.VMEM((tiles, width + count, height), F32),
+            pltpu.VMEM((tiles, width + count, height), BF16),
+            pltpu.VMEM((tiles, width, height), F32),
             pltpu.VMEM((group1 * channels, 3 * (group1 + 2) * cin), BF16),
             pltpu.VMEM((group2 * channels, 3 * (group2 + 2) * channels), BF16),
             pltpu.VMEM((channels, 128), F32),

time: 72.4 us -> 65.5 us (0.905)
  Pallas kernels: 67.9 us -> 61 us
    pallas_call x1, Pallas kernels: 65.7 us -> 58.7 us  [local(): pl.pallas_call(partial(main_kernel, count, group1, group2), in_specs=[vme...]
where the time goes in v3:
time: 65.5 us; the launch traced here: 65.2 us
  Pallas kernels  61 us (93%)
  local copies, waits for them, and re-layouts  2.95 us (5%)
  between operations  1.29 us (2%)
    pallas_call x1, Pallas kernels, local(): pl.pallas_call(partial(main_kernel, count, group1, group2), in_specs=[vme...  58.7 us
    pallas_call x1, Pallas kernels, local(): pl.pallas_call(drain_kernel, out_shape=jax.ShapeDtypeStruct((width + coun...  2.27 us
    reshape x1, local copies, waits for them, and re-layouts, local(): jnp.transpose(blocks, (1, 0, 2, 3))  1.65 us

profile of v3, /device:TPU:0, one launch (start us, length us, event | category | flops | bytes accessed | tf_op | source)
XLA Modules:
  0.0 65.2 jit_solution(16889000603869992752)
XLA Ops:
  1.3 2.3 %shard_map.104.packed_ref = bf16[96,128]{1,0:T(8,128)(2,1)} custom-call(s32[64,128]{1,0:T(8,128)} %codes_ref.1, s32[1,32]{1,0:T(1,128)} %outlets_ref.1, s32[1,32]{1,0:T(1,128)} %receivers_ref.1, s32[1,32]{1,0:T(1,128)} %inlets_ref.1, s32[1]{0:T(128)S(6)} %copy.15.levels_ref), custom_call_target="tpu_custom_call" | custom-call | tf_op jit(solution)/shard_map/pallas_call | solution.py:463
  3.6 58.7 %shard_map.105 = (bf16[8,12,8,128]{3,2,1,0:T(8,128)(2,1)}, f32[16,128]{1,0:T(8,128)}) custom-call(bf16[12,8,16,1024]{3,2,1,0:T(8,128)(2,1)} %forcing_ref.1, bf16[3,3,16,64]{3,2,1,0:T(8,128)(2,1)} %first_ref.1, bf16[3,3,64,64]{3,2,1,0:T(8,128)(2,1)} %second_ref.1, bf16[1,64]{1,0:T(2,128)(2,1)} %bitcast.10, bf16[96,128]{1,0:T(8,128)(2,1)} %shard_map.104.packed_ref), custom_call_target="tpu_custom_call" | custom-call | tf_op jit(solution)/shard_map/pallas_call | solution.py:474
  62.3 1.7 %copy_bitcast_fusion = bf16[12,64,128]{2,1,0:T(8,128)(2,1)} fusion(bf16[8,12,8,128]{3,2,1,0:T(8,128)(2,1)} %get-tuple-element.4), kind=kLoop, calls=%fused_computation | loop fusion | bytes 393216 | tf_op jit(solution)/shard_map/reshape | solution.py:510
  63.9 0.7 %slice_bitcast_fusion = f32[1,32,12]{1,2,0:T(8,128)S(1)} fusion(f32[16,128]{1,0:T(8,128)} %get-tuple-element.5), kind=kLoop, calls=%fused_computation.1 | loop fusion | bytes 3072 | tf_op jit(solution)/shard_map/broadcast_in_dim | solution.py:511
  64.6 0.6 copy.13
